TPU v7x, 512 devices: a whole 4x4x16 slice. The times are simulated.
512 devices in a mesh: batch: 16 (over y, z_hi), proto: 32 (over x, z_lo, core).
Axes of the slice: x: 4, y: 4, z: 16 (z_hi: 4, z_lo: 4; z = z_hi * 4 + z_lo), core: 2. Of those that a mesh axis runs over, the one named last changes fastest.
Arguments:
- teacher_feats: bfloat16 [8192, 1536], P('batch'), may hold values from -8 to 8
- teacher_weight: bfloat16 [1536, 32768], P('batch', 'proto'), may hold values from -1 to 1
- student_feats: bfloat16 [8192, 1024], P('batch'), may hold values from -6 to 6
- student_weight: bfloat16 [1024, 32768], P('batch', 'proto'), may hold values from -3 to 3
Outputs:
- loss: float32 [], replicated
- grad_student_weight: bfloat16 [1024, 32768], P('batch', 'proto')
- grad_student_feats: bfloat16 [8192, 1024], P('batch')
All inputs are finite; a program needn't handle non-finite values.
Results may differ from a plain program's by a relative error of at most 0.0082.
Values may be sent and summed in bfloat16 or wider, within the bound.
A program may use at most 64 MiB of HBM per device.

v0:
```python
import jax
import jax.numpy as jnp
from jax import lax
from jax.sharding import PartitionSpec as P

ROUNDS = 3


teacher_temp = 0.07
student_temp = 0.1
loss_scale = 1024.0


def swapped(x, axis, bit):
    return lax.ppermute(x, axis, [(i, i ^ 1 << bit) for i in range(lax.axis_size(axis))])


def unit_rows(values):
    wide = values.astype(jnp.float32)
    scale = lax.rsqrt(jnp.sum(wide * wide, axis=1, keepdims=True) + 1e-06)
    return (wide * scale, scale)


def shards(teacher_feats, teacher_weight, student_feats, student_weight):
    rows_here = teacher_feats.shape[0]
    protos_here = teacher_weight.shape[1]
    crops = rows_here * lax.axis_size("batch")
    protos = protos_here * lax.axis_size("proto")
    half_bit = lax.axis_size("batch").bit_length() - 2
    teacher_unit, _ = unit_rows(teacher_feats)
    teacher_half = teacher_unit.astype(jnp.bfloat16)
    columns = teacher_half
    scores = jnp.dot(
        columns,
        lax.all_gather(teacher_weight, "batch", axis=0, tiled=True),
        preferred_element_type=jnp.float32,
    )
    mass = jnp.exp(scores / teacher_temp)
    for step in range(ROUNDS):
        column_total = lax.psum(jnp.sum(mass, axis=0), "batch")
        mass = mass / (protos * column_total[None, :])
        row_total = lax.psum(jnp.sum(mass, axis=1), "proto")
        mass = mass / (crops * row_total[:, None])
    targets = (mass * crops).astype(jnp.bfloat16)
    targets = swapped(targets, "batch", half_bit)
    relayed = targets.astype(jnp.float32)
    student_unit, scale = unit_rows(student_feats)
    student_half = student_unit.astype(jnp.bfloat16)
    weight_full = lax.all_gather(student_weight, "batch", axis=0, tiled=True)
    logits = jnp.dot(student_half, weight_full, preferred_element_type=jnp.float32) / student_temp
    expo = jnp.exp(logits)
    local_weight = jnp.sum(relayed, axis=1)
    total, weight_sum = lax.psum((jnp.sum(expo, axis=1), local_weight), "proto")
    loss_term = jnp.sum(local_weight * jnp.log(total) - jnp.sum(relayed * logits, axis=1))
    loss = lax.psum(loss_term, ("batch", "proto")) / crops
    slope = (
        loss_scale * (weight_sum[:, None] * expo / total[:, None] - relayed) / student_temp
    ).astype(jnp.bfloat16)
    columns = student_half
    grad_weight = lax.psum_scatter(
        lax.dot_general(
            columns, slope, (((0,), (0,)), ((), ())), preferred_element_type=jnp.float32
        ),
        "batch",
        scatter_dimension=0,
        tiled=True,
    ).astype(jnp.bfloat16)
    partial_back = lax.dot_general(
        slope, weight_full, (((1,), (1,)), ((), ())), preferred_element_type=jnp.float32
    )
    back = lax.psum(partial_back, "proto")
    inner = jnp.sum(student_unit * back, axis=1, keepdims=True)
    grad_feats = ((back - student_unit * inner) * scale).astype(jnp.bfloat16)
    return (loss, grad_weight, grad_feats)


def solution(mesh):
    return jax.shard_map(
        shards,
        mesh=mesh,
        in_specs=(P("batch", None), P("batch", "proto"), P("batch", None), P("batch", "proto")),
        out_specs=(P(), P("batch", "proto"), P("batch", None)),
        check_vma=False,
    )
```

profile of v0, /device:TPU:1, one launch (start us, length us, event | category | flops | bytes accessed | tf_op | source)
XLA Modules:
  0.0 1061.3 jit_solution(8003824956656104335)
XLA Ops:
  7.2 0.7 all-gather.3.cloned.1.call-update
  7.9 0.7 all-gather.5.cloned.1.call-update
  8.7 1.8 fusion
  10.5 121.0 %all-gather.3.cloned.1.call-done = bf16[1536,1024]{1,0:T(8,128)(2,1)} async-done(((bf16[96,1024]{1,0:T(8,128)(2,1)}), bf16[1536,1024]{1,0:T(8,128)(2,1)}) %all-gather.3.cloned.1.call-update) | async-done | bytes 3145744 | tf_op jit(solution)/shard_map/all_gather | solution.py:35
  131.5 4.2 fusion.32
  135.7 45.5 %psum.70 = f32[1024]{0:T(1024)S(1)} all-reduce(f32[1024]{0:T(1024)S(1)} %get-tuple-element.8), channel_id=1, replica_groups=mesh['batch'=16,'proto'=32] {'batch'}, use_global_device_ids=true, to_apply=%region_2.0 | all-reduce | flops 1024 | bytes 8192 | tf_op jit(solution)/shard_map/psum | solution.py:40
  181.2 0.2 divide_reduce_fusion
  181.4 80.1 %psum.71 = f32[512]{0:T(512)S(1)} all-reduce(f32[512]{0:T(512)S(1)} %divide_reduce_fusion), channel_id=1, replica_groups=mesh['batch'=16,'proto'=32] {'proto'}, use_global_device_ids=true, to_apply=%region_4.0 | all-reduce | flops 512 | bytes 4096 | tf_op jit(solution)/shard_map/psum | solution.py:42
  261.6 0.4 fusion.21
  261.9 44.4 %psum.72 = f32[1024]{0:T(1024)S(1)} all-reduce(f32[1024]{0:T(1024)S(1)} %fusion.21), channel_id=1, replica_groups=mesh['batch'=16,'proto'=32] {'batch'}, use_global_device_ids=true, to_apply=%region_6.0 | all-reduce | flops 1024 | bytes 8192 | tf_op jit(solution)/shard_map/psum | solution.py:40
  306.3 0.5 fusion.23
  306.8 78.3 %psum.73 = f32[512]{0:T(512)S(1)} all-reduce(f32[512]{0:T(512)S(1)} %fusion.23), channel_id=1, replica_groups=mesh['batch'=16,'proto'=32] {'proto'}, use_global_device_ids=true, to_apply=%region_8.0 | all-reduce | flops 512 | bytes 4096 | tf_op jit(solution)/shard_map/psum | solution.py:42
  385.2 0.5 fusion.24
  385.7 39.3 %psum.74 = f32[1024]{0:T(1024)S(1)} all-reduce(f32[1024]{0:T(1024)S(1)} %fusion.24), channel_id=1, replica_groups=mesh['batch'=16,'proto'=32] {'batch'}, use_global_device_ids=true, to_apply=%region_10.0 | all-reduce | flops 1024 | bytes 8192 | tf_op jit(solution)/shard_map/psum | solution.py:40
  425.0 0.7 fusion.25
  425.7 74.5 %psum.75 = f32[512]{0:T(512)S(1)} all-reduce(f32[512]{0:T(512)S(1)} %fusion.25), channel_id=1, replica_groups=mesh['batch'=16,'proto'=32] {'proto'}, use_global_device_ids=true, to_apply=%region_12.0 | all-reduce | flops 512 | bytes 4096 | tf_op jit(solution)/shard_map/psum | solution.py:42
  500.2 1.7 fusion.22
  501.9 1.9 collective-permute-start
  503.8 0.3 fusion.15
  504.2 25.4 %collective-permute-done = bf16[512,1024]{1,0:T(8,128)(2,1)S(1)} collective-permute-done((bf16[512,1024]{1,0:T(8,128)(2,1)}, bf16[512,1024]{1,0:T(8,128)(2,1)S(1)}, u32[]{:S(2)}, u32[]{:S(2)}) %collective-permute-start) | collective-permute-done | bytes 1048608 | tf_op jit(solution)/shard_map/ppermute | solution.py:15
  529.6 4.5 exponential_reduce_fusion
  534.0 68.2 %all-reduce = (f32[512]{0:T(512)S(1)}, f32[512]{0:T(512)S(1)}) all-reduce(f32[512]{0:T(512)S(1)} %get-tuple-element.3, f32[512]{0:T(512)S(1)} %get-tuple-element.5), channel_id=1, replica_groups=mesh['batch'=16,'proto'=32] {'proto'}, use_global_device_ids=true, to_apply=%region_16.0 | all-reduce | flops 1024 | bytes 8192 | tf_op jit(solution)/shard_map/psum | solution.py:53
  602.3 2.4 fusion.20
  604.6 2.6 fusion.33
  607.3 3.3 fusion.28
  610.7 0.6 subtract_reduce_fusion
  611.3 100.3 %psum.77 = f32[]{:T(128)} all-reduce(f32[]{:T(128)} %subtract_reduce_fusion), channel_id=1, replica_groups=mesh['batch'=16,'proto'=32] {'batch','proto'}, use_global_device_ids=true, to_apply=%region_19.0 | all-reduce | flops 1 | bytes 8 | tf_op jit(solution)/shard_map/psum | solution.py:55
  712.2 179.9 %all-reduce.3.cloned.1.call-done = f32[512,1024]{1,0:T(8,128)} async-done(((f32[512,1024]{1,0:T(8,128)}), f32[512,1024]{1,0:T(8,128)}) %all-reduce.3.cloned.1.call-update) | async-done | bytes 2097168 | tf_op jit(solution)/shard_map/psum | solution.py:71
  892.2 2.2 fusion.11
  894.4 1.4 fusion.14
  895.8 156.2 %reduce-scatter.2.cloned.1.call-done = f32[64,1024]{1,0:T(8,128)} async-done(((f32[1024,1024]{1,0:T(8,128)}), f32[64,1024]{1,0:T(8,128)}) %reduce-scatter.2.cloned.1.call-update) | async-done | bytes 262160 | tf_op jit(solution)/shard_map/reduce_scatter | solution.py:60
  1052.0 1.6 convert_element_type.34
  (21 shorter events, 0.3 us)
Async XLA Ops:
  7.2 124.3 %all-gather.3.cloned.1.call-start = ((), (), s32[]{:S(2)}) async-start(), calls=%async_computation.1 | async-start | bytes 3342336 | tf_op jit(solution)/shard_map/all_gather | solution.py:35
  7.9 496.3 %all-gather.5.cloned.1.call-start = ((), (), s32[]{:S(2)}) async-start(), calls=%async_computation.2 | async-start | bytes 2228224 | tf_op jit(solution)/shard_map/all_gather | solution.py:49
  8.6 883.5 %all-reduce.3.cloned.1.call-start = ((), (), s32[]{:S(2)}) async-start(), calls=%async_computation.4 | async-start | bytes 4194304 | tf_op jit(solution)/shard_map/psum | solution.py:71
  425.7 78.1 %copy-start = (bf16[512,1024]{1,0:T(8,128)(2,1)S(1)}, bf16[512,1024]{1,0:T(8,128)(2,1)}, u32[]{:S(2)}) copy-start(bf16[512,1024]{1,0:T(8,128)(2,1)} %param.6) | copy-start | bytes 3145732
  501.9 27.7 %collective-permute-start = (bf16[512,1024]{1,0:T(8,128)(2,1)}, bf16[512,1024]{1,0:T(8,128)(2,1)S(1)}, u32[]{:S(2)}, u32[]{:S(2)}) collective-permute-start(bf16[512,1024]{1,0:T(8,128)(2,1)} %fusion.22), channel_id=1, source_target_pairs={{0,256},{32,288},{64,320},{96,352},{128,384},{160,416},{192,448},{... | collective-permute-start | bytes 3145736 | tf_op jit(solution)/shard_map/ppermute | solution.py:15
  602.3 2.4 copy-start.2
  607.3 444.7 %reduce-scatter.2.cloned.1.call-start = ((), (), s32[]{:S(2)}) async-start(), calls=%async_computation.3 | async-start | bytes 4456448 | tf_op jit(solution)/shard_map/reduce_scatter | solution.py:60
  892.2 2.2 copy-start.1
Sparse Core Ops, SparseCore 0:
  11.1 120.3 all-gather.2
  134.5 90.8 all-gather.4
  607.4 284.6 all-reduce.2
  896.8 155.1 reduce-scatter.1
where the time goes:
time: 1060 us
  blocking collectives  531 us (50%)
  waiting for transfers between devices  484 us (46%)
  between operations  15.6 us (1%)
  matrix products  14.6 us (1%)
  other arithmetic  14.3 us (1%)
    psum x3, blocking collectives, shards(): row_total = lax.psum(jnp.sum(mass, axis=1), 'proto')  233 us
    psum x1, waiting for transfers between devices, shards(): back = lax.psum(partial_back, 'proto')  180 us
    reduce_scatter x1, waiting for transfers between devices, shards(): lax.psum_scatter(lax.dot_general(columns, slope, (((0,), (0,)), ((), ()))...  156 us
    psum x3, blocking collectives, shards(): column_total = lax.psum(jnp.sum(mass, axis=0), 'batch')  129 us
    all_gather x1, waiting for transfers between devices, shards(): lax.all_gather(teacher_weight, 'batch', axis=0, tiled=True)  121 us
    psum x1, blocking collectives, shards(): loss = lax.psum(loss_term, ('batch', 'proto')) / crops  100 us
    psum x1, blocking collectives, shards(): total, weight_sum = lax.psum((jnp.sum(expo, axis=1), local_weight), 'proto')  68.2 us
    ppermute x1, waiting for transfers between devices, swapped(): lax.ppermute(x, axis, [(i, i ^ 1 << bit) for i in range(lax.axis_size(axi...  25.4 us
  transfers between devices with their start and end apart: 5, of which 4 were waited for; matrix products, arithmetic and copies ran while one was open for 2% of the time, Pallas kernels for 0%

commit v1 on v0

v1 whole, which is shorter than its diff:
```python
import jax
import jax.numpy as jnp
from jax import lax
from jax.experimental import pallas as pl
from jax.experimental.pallas import tpu as pltpu
from jax.sharding import PartitionSpec as P

F32 = jnp.float32
BF16 = jnp.bfloat16
MESH = pl.DeviceIdType.MESH

TEACHER_TEMP = 0.07
STUDENT_TEMP = 0.1
LOSS_SCALE = 1024.0
CROPS = 8192.0
PROTOS = 32768.0
GAIN = LOSS_SCALE / STUDENT_TEMP

ROWS = 512
COLS = 1024
DT = 1536
DS = 1024
NSEM = 160


def device(y, zh, x, zl, c):
    return (y * 4 + zh, (x * 4 + zl) * 2 + c)


def nt(a, b):
    return lax.dot_general(a, b, (((1,), (1,)), ((), ())), preferred_element_type=F32)


def lanes(part):
    ones = jnp.ones((8, 128), F32)
    out = lax.dot_general(
        ones, part, (((1,), (1,)), ((), ())),
        precision=lax.Precision.HIGHEST, preferred_element_type=F32,
    )
    return out[0:1, :]


def inverse(value, gain):
    part = jnp.where(value > 1.0, 0.25, 1.0)
    return (1.0 / (value * part)) * (part * gain)


def kernel(
    tf, tw, sf, sw, loss_out, gw_out, gf_out,
    tu, wt, ws, sf2, sh, sht, mass, logit, expo, slope,
    rowpart, totpart, rowb, probb,
    colmsg, colbuf, rowmsg, rowbuf, lastmsg, lastbuf,
    lossmsg, lossrow, losscol,
    bsend, bown, brecv, xsend, xrecv, lsend, lrecv, gfin, gfs,
    gsend, gown, grecv, zsend, zown, zrecv,
    ssem, rsem,
):
    b = lax.axis_index("batch")
    p = lax.axis_index("proto")
    y, zh = b // 4, b % 4
    x, zl, c = p // 8, (p // 2) % 4, p % 2

    def at_y(d):
        return lax.rem(y + d, 4)

    def at_zh(d):
        return lax.rem(zh + d, 4)

    def at_x(d):
        return lax.rem(x + d, 4)

    used = [0]
    pending = []

    def sem():
        used[0] += 1
        return used[0] - 1

    def send(src, dst, dev, s=None, r=None):
        s = sem() if s is None else s
        r = s if r is None else r
        copy = pltpu.make_async_remote_copy(
            src_ref=src, dst_ref=dst, send_sem=ssem.at[s], recv_sem=rsem.at[r],
            device_id=dev, device_id_type=MESH,
        )
        copy.start()
        return copy

    def single(src, dst, dev):
        copy = send(src, dst, dev)
        pending.append(copy.wait_send)
        return copy

    def wait_bytes(ref, s):
        pltpu.make_async_copy(ref, ref, s).wait()

    def batch_send(src, buf):
        s = sem()
        for dz in (2, 1, 3, 0):
            for dy in (2, 1, 3, 0):
                if dy or dz:
                    send(src, buf.at[dy * 4 + dz - 1], device(at_y(dy), at_zh(dz), x, zl, c), s)
        pending.append(lambda: wait_bytes(buf, ssem.at[s]))
        return lambda: wait_bytes(buf, rsem.at[s])

    def proto_send(src, buf):
        s = sem()

        def body(i, carry):
            k = 31 - i
            dx, dl, dc = k // 8, (k // 2) % 4, k % 2
            fl = lax.rem(zl + dl, 4)
            send(src, buf.at[k - 1], device(y, zh, at_x(dx), fl, lax.rem(c + dc, 2)), s)
            return carry

        lax.fori_loop(0, 31, body, 0)
        pending.append(lambda: wait_bytes(buf, ssem.at[s]))
        return lambda: wait_bytes(buf, rsem.at[s])

    near = [device(at_y(d), zh, x, zl, c) for d in (1, 2, 3)]
    near += [device(y, at_zh(d), x, zl, c) for d in (1, 2, 3)]
    near += [device(y, zh, x, lax.rem(zl + d, 4), c) for d in (1, 2, 3)]
    near += [
        device(y, zh, at_x(d), zl, lax.rem(c + e, 2))
        for d in range(4) for e in range(2) if d or e
    ]
    barrier = pltpu.get_barrier_semaphore()
    for dev in near:
        pl.semaphore_signal(barrier, inc=1, device_id=dev, device_id_type=MESH)

    def own(block, size):
        return pl.ds(pl.multiple_of(block * size, 16), size)

    wt[own(b, 96), :] = tw[...]
    ws[own(b, 64), :] = sw[...]
    pl.semaphore_wait(barrier, len(near))

    def gather(full, rows):
        half = rows // 2

        def part(dy, dz, h):
            start = (at_y(dy) * 4 + at_zh(dz)) * rows + h * half
            return full.at[pl.ds(pl.multiple_of(start, 16), half), :]

        zcopy, ycopy = {}, {}

        def zsend_(dz_src, h, way):
            ref = part(0, dz_src, h)
            zcopy[(dz_src, h, way)] = single(ref, ref, device(y, at_zh(way), x, zl, c))

        def ysend_(dy_src, dz, h, way):
            ref = part(dy_src, dz, h)
            ycopy[(dy_src, dz, h, way)] = single(ref, ref, device(at_y(way), zh, x, zl, c))

        return zsend_, ysend_, zcopy, ycopy

    tz, ty, tzc, tyc = gather(wt, 96)
    sz, sy, szc, syc = gather(ws, 64)

    def y_both(ysend_, dz):
        for h in (0, 1):
            ysend_(0, dz, h, 1)
            ysend_(0, dz, h, 3)

    def y_forward(ysend_, yc, dz, h):
        if h == 0:
            yc[(0, dz, 0, 1)].wait_recv()
            ysend_(3, dz, 0, 1)
        else:
            yc[(0, dz, 1, 3)].wait_recv()
            ysend_(1, dz, 1, 3)

    tz(0, 0, 1)
    tz(0, 1, 3)
    tz(0, 1, 1)
    tz(0, 0, 3)
    slice_rows = pl.ds(pl.multiple_of((2 * x + c) * 64, 64), 64)
    swap = single(sf.at[slice_rows, :], sf2.at[slice_rows, :], device(at_y(2), zh, x, zl, c))
    y_both(ty, 0)

    def teacher_rows(i, carry):
        rows = pl.ds(pl.multiple_of(i * 128, 128), 128)
        wide = tf[rows, :].astype(F32)
        scale = lax.rsqrt(jnp.sum(wide * wide, axis=1, keepdims=True) + 1e-06)
        tu[rows, :] = (wide * scale).astype(BF16)
        return carry

    lax.fori_loop(0, 4, teacher_rows, 0)

    swap.wait_recv()
    s_feats = sem()
    for d in range(4):
        for e in range(2):
            if d or e:
                send(
                    sf2.at[slice_rows, :], sf2.at[slice_rows, :],
                    device(y, zh, at_x(d), zl, lax.rem(c + e, 2)), s_feats,
                )
    rest = sf2.at[pl.ds(0, 448), :]
    pending.append(lambda: wait_bytes(rest, ssem.at[s_feats]))

    y_forward(ty, tyc, 0, 0)
    y_forward(ty, tyc, 0, 1)
    tzc[(0, 0, 1)].wait_recv()
    tz(3, 0, 1)
    ty(0, 3, 0, 1)
    ty(0, 3, 0, 3)
    tzc[(0, 1, 3)].wait_recv()
    tz(1, 1, 3)
    ty(0, 1, 1, 1)
    ty(0, 1, 1, 3)
    sz(0, 0, 1)
    sz(0, 1, 3)
    sz(0, 1, 1)
    sz(0, 0, 3)
    y_forward(ty, tyc, 3, 0)
    y_forward(ty, tyc, 1, 1)
    tzc[(0, 1, 1)].wait_recv()
    ty(0, 3, 1, 1)
    ty(0, 3, 1, 3)
    tzc[(0, 0, 3)].wait_recv()
    ty(0, 1, 0, 1)
    ty(0, 1, 0, 3)
    y_forward(ty, tyc, 3, 1)
    y_forward(ty, tyc, 1, 0)
    tzc[(3, 0, 1)].wait_recv()
    ty(0, 2, 0, 1)
    ty(0, 2, 0, 3)
    tzc[(1, 1, 3)].wait_recv()
    ty(0, 2, 1, 1)
    ty(0, 2, 1, 3)
    y_both(sy, 0)

    wait_bytes(rest, rsem.at[s_feats])

    def student_rows(i, carry):
        rows = pl.ds(pl.multiple_of(i * 128, 128), 128)
        wide = sf2[rows, :].astype(F32)
        scale = lax.rsqrt(jnp.sum(wide * wide, axis=1, keepdims=True) + 1e-06)
        unit = wide * scale
        sh[rows, :] = unit.astype(BF16)
        sht[:, rows] = unit.T.astype(BF16)
        return carry

    lax.fori_loop(0, 4, student_rows, 0)

    y_forward(ty, tyc, 2, 0)
    y_forward(ty, tyc, 2, 1)
    for dz in (0, 3, 1, 2):
        tyc[(0, dz, 1, 1)].wait_recv()
        tyc[(0, dz, 0, 3)].wait_recv()
        tyc[(3, dz, 0, 1)].wait_recv()
        tyc[(1, dz, 1, 3)].wait_recv()

    def score_cols(j, carry):
        cols = pl.ds(pl.multiple_of(j * 256, 256), 256)
        scores = jnp.dot(tu[...], wt[:, cols], preferred_element_type=F32)
        block = jnp.exp(scores / TEACHER_TEMP)
        mass[:, cols] = block
        colmsg[0, :, cols] = jnp.sum(block, axis=0, keepdims=True)
        return carry

    lax.fori_loop(0, 4, score_cols, 0)

    def by_columns(factor, after):
        def body(i, carry):
            rows = pl.ds(pl.multiple_of(i * 64, 64), 64)
            part = jnp.zeros((64, 128), F32)
            for t in range(8):
                cols = slice(128 * t, 128 * t + 128)
                block = mass[rows, cols] * factor[:, cols]
                if after != 1.0:
                    block = block * after
                mass[rows, cols] = block
                part = part + block
            rowpart[rows, :] = part
            return carry

        lax.fori_loop(0, 8, body, 0)
        return lanes(rowpart[...])

    def by_rows(factor):
        rowb[...] = jnp.broadcast_to(factor, (128, ROWS)).T

        def body(i, carry):
            rows = pl.ds(pl.multiple_of(i * 64, 64), 64)
            by = rowb[rows, :]
            out = []
            for t in range(8):
                cols = slice(128 * t, 128 * t + 128)
                block = mass[rows, cols] * by
                mass[rows, cols] = block
                out.append(carry[t] + jnp.sum(block.reshape(8, 8, 128), axis=0))
            return tuple(out)

        sums = lax.fori_loop(0, 8, body, tuple(jnp.zeros((8, 128), F32) for _ in range(8)))
        return jnp.concatenate([jnp.sum(s, axis=0, keepdims=True) for s in sums], axis=1)

    def total_of(msg, buf):
        return msg + jnp.sum(buf[...], axis=0)

    def student_logits():
        def body(j, carry):
            cols = pl.ds(pl.multiple_of(j * 256, 256), 256)
            block = jnp.dot(sh[...], ws[:, cols], preferred_element_type=F32) / STUDENT_TEMP
            grown = jnp.exp(block)
            logit[:, cols] = block
            expo[:, cols] = grown
            part = grown[:, :128] + grown[:, 128:]
            totpart[...] = jnp.where(j == 0, part, totpart[...] + part)
            return carry

        lax.fori_loop(0, 4, body, 0)

    def student_near():
        szc[(0, 0, 1)].wait_recv()
        sz(3, 0, 1)
        szc[(0, 1, 3)].wait_recv()
        sz(1, 1, 3)
        for dz, h in ((3, 0), (1, 1)):
            sy(0, dz, h, 1)
            sy(0, dz, h, 3)
        y_forward(sy, syc, 0, 0)
        y_forward(sy, syc, 0, 1)
        szc[(0, 1, 1)].wait_recv()
        szc[(0, 0, 3)].wait_recv()
        for dz, h in ((3, 1), (1, 0)):
            sy(0, dz, h, 1)
            sy(0, dz, h, 3)

    def student_far():
        szc[(3, 0, 1)].wait_recv()
        szc[(1, 1, 3)].wait_recv()
        y_both(sy, 2)
        y_forward(sy, syc, 3, 0)
        y_forward(sy, syc, 1, 1)
        y_forward(sy, syc, 3, 1)
        y_forward(sy, syc, 1, 0)

    def student_last():
        y_forward(sy, syc, 2, 0)
        y_forward(sy, syc, 2, 1)

    def student_end():
        for dz in (0, 3, 1, 2):
            syc[(0, dz, 1, 1)].wait_recv()
            syc[(0, dz, 0, 3)].wait_recv()
            syc[(3, dz, 0, 1)].wait_recv()
            syc[(1, dz, 1, 3)].wait_recv()
        student_logits()

    for step in range(3):
        got = batch_send(colmsg.at[step], colbuf.at[step])
        if step == 0:
            student_near()
        if step == 1:
            student_last()
        if step == 2:
            student_end()
            lastmsg[:, 512:] = lanes(totpart[...])
        got()
        col_total = total_of(colmsg[step], colbuf.at[step]) * PROTOS
        if step == 0:
            factor = 1.0 / (col_total * 0.25)
            row_sum = by_columns(factor, 0.25)
        else:
            row_sum = by_columns(1.0 / col_total, 1.0)
        if step < 2:
            rowmsg[step] = row_sum
            got = proto_send(rowmsg.at[step], rowbuf.at[step])
            if step == 0:
                student_far()
            got()
            row_total = total_of(rowmsg[step], rowbuf.at[step])
            colmsg[step + 1] = by_rows(1.0 / (CROPS * row_total))
        else:
            lastmsg[:, :512] = row_sum
            got = proto_send(lastmsg, lastbuf)
            got()
    both = total_of(lastmsg[...], lastbuf)
    row_total, total = both[:, :512], both[:, 512:]
    target_factor = CROPS * (1.0 / (CROPS * row_total))
    weight_sum = target_factor * row_total
    rowb[...] = jnp.broadcast_to(target_factor, (128, ROWS)).T
    probb[...] = jnp.broadcast_to(weight_sum * inverse(total, GAIN), (128, ROWS)).T
    crop_term = jnp.sum(weight_sum * jnp.log(total), axis=1, keepdims=True) / 32.0

    def slope_rows(i, carry):
        rows = pl.ds(pl.multiple_of(i * 64, 64), 64)
        by, prob = rowb[rows, :], probb[rows, :]
        for t in range(8):
            cols = slice(128 * t, 128 * t + 128)
            target = mass[rows, cols] * by
            slope[rows, cols] = (expo[rows, cols] * prob - target * GAIN).astype(BF16)
            carry = carry + jnp.sum((target * logit[rows, cols]).reshape(8, 8, 128), axis=0)
        return carry

    pairs = lax.fori_loop(0, 8, slope_rows, jnp.zeros((8, 128), F32))
    pairs = jnp.sum(jnp.sum(pairs, axis=0, keepdims=True), axis=1, keepdims=True)
    lossmsg[0] = jnp.broadcast_to(crop_term - pairs, (1, 128))

    def back_half(half, store):
        rows = pl.ds(pl.multiple_of(half * 256, 256), 256)

        def body(j, carry):
            feats = pl.ds(pl.multiple_of(j * 256, 256), 256)
            store(feats, nt(slope[rows, :], ws[feats, :]))
            return carry

        lax.fori_loop(0, 4, body, 0)

    def store_send(feats, value):
        bsend[:, feats] = value.astype(BF16)

    def store_own(feats, value):
        bown[:, feats] = value

    back_half(1 - c, store_send)
    core_copy = single(bsend, brecv, device(y, zh, x, zl, 1 - c))

    ycopies = []
    for q in range(4):
        cols = slice(256 * q, 256 * q + 256)
        copies = []
        for dy in (2, 1, 3, 0):
            rows = pl.ds(pl.multiple_of(at_y(dy) * 256, 256), 256)
            value = jnp.dot(sht[rows, :], slope[:, cols], preferred_element_type=F32)
            if dy:
                gsend[q, dy - 1] = value.astype(BF16)
                copies.append(
                    single(gsend.at[q, dy - 1], grecv.at[q, dy - 1], device(at_y(dy), zh, x, zl, c))
                )
            else:
                gown[q] = value
        ycopies.append(copies)
        if q == 0:
            back_half(c, store_own)

    loss_got = proto_send(lossmsg.at[0], lossrow)

    core_copy.wait_recv()
    xcopies = []
    for d in (2, 1, 3):
        rows = pl.ds(pl.multiple_of(at_x(d) * 64, 64), 64)
        xsend[d - 1] = (bown[rows, :] + brecv[rows, :].astype(F32)).astype(BF16)
        xcopies.append(single(xsend.at[d - 1], xrecv.at[d - 1], device(y, zh, at_x(d), zl, c)))

    zcopies = []

    def weight_z(q):
        for copy in ycopies[q]:
            copy.wait_recv()
        copies = []
        for dz in (2, 1, 3, 0):
            rows = pl.ds(pl.multiple_of(at_zh(dz) * 64, 64), 64)
            value = gown[q, rows, :]
            for d in range(3):
                value = value + grecv[q, d, rows, :].astype(F32)
            if dz:
                zsend[q, dz - 1] = value.astype(BF16)
                copies.append(
                    single(zsend.at[q, dz - 1], zrecv.at[q, dz - 1], device(y, at_zh(dz), x, zl, c))
                )
            else:
                zown[q] = value
        zcopies.append(copies)

    weight_z(0)

    for copy in xcopies:
        copy.wait_recv()
    rows = pl.ds(pl.multiple_of(x * 64, 64), 64)
    xsum = bown[rows, :] + brecv[rows, :].astype(F32)
    for d in range(3):
        xsum = xsum + xrecv[d].astype(F32)
    bown[pl.ds(0, 64), :] = xsum
    lcopies = []
    for d in (2, 1, 3):
        fl = lax.rem(zl + d, 4)
        rows = pl.ds(pl.multiple_of(fl * 16, 16), 16)
        lsend[d - 1] = bown[rows, :].astype(BF16)
        lcopies.append(single(lsend.at[d - 1], lrecv.at[d - 1], device(y, zh, x, fl, c)))

    weight_z(1)
    loss_got()
    lossmsg[1] = lossmsg[0] + jnp.sum(lossrow[...], axis=0)
    loss_got = batch_send(lossmsg.at[1], losscol)

    for copy in lcopies:
        copy.wait_recv()
    rows = pl.ds(pl.multiple_of(zl * 16, 16), 16)
    back = bown[rows, :]
    for d in range(3):
        back = back + lrecv[d].astype(F32)
    mine = pl.ds(pl.multiple_of(c * 256 + x * 64 + zl * 16, 16), 16)
    wide = sf2[mine, :].astype(F32)
    scale = lax.rsqrt(jnp.sum(wide * wide, axis=1, keepdims=True) + 1e-06)
    unit = wide * scale
    inner = jnp.sum(unit * back, axis=1, keepdims=True)
    gfin[...] = ((back - unit * inner) * scale).astype(BF16)
    fcopies = []
    for d in range(4):
        fl = lax.rem(zl + d, 4)
        fcopies.append(single(gfin, gfs.at[mine, :], device(at_y(2), zh, x, fl, c)))

    weight_z(2)

    for copy in fcopies:
        copy.wait_recv()

    def piece(dx, core):
        return gfs.at[pl.ds(pl.multiple_of(core * 256 + at_x(dx) * 64, 64), 64), :]

    lastx = []
    for d in (2, 1, 3):
        lastx.append(single(piece(0, c), piece(0, c), device(y, zh, at_x(d), zl, c)))
    lastc = [single(piece(0, c), piece(0, c), device(y, zh, x, zl, 1 - c))]

    weight_z(3)

    for d, copy in zip((2, 1, 3), lastx):
        copy.wait_recv()
        lastc.append(single(piece(4 - d, c), piece(4 - d, c), device(y, zh, x, zl, 1 - c)))

    for q in range(4):
        cols = slice(256 * q, 256 * q + 256)
        for copy in zcopies[q]:
            copy.wait_recv()
        value = zown[q]
        for d in range(3):
            value = value + zrecv[q, d].astype(F32)
        gw_out[:, cols] = value.astype(BF16)

    loss_got()
    loss_out[...] = (lossmsg[1] + jnp.sum(losscol[...], axis=0)) / CROPS

    for copy in lastc:
        copy.wait_recv()
    gf_out[...] = gfs[...]
    for done in pending:
        done()


def shards(teacher_feats, teacher_weight, student_feats, student_weight):
    vm = pltpu.VMEM
    spec = pl.BlockSpec(memory_space=pltpu.VMEM)
    loss, grad_weight, grad_feats = pl.pallas_call(
        kernel,
        out_shape=(
            jax.ShapeDtypeStruct((1, 128), F32),
            jax.ShapeDtypeStruct((64, COLS), BF16),
            jax.ShapeDtypeStruct((ROWS, DS), BF16),
        ),
        in_specs=[spec] * 4,
        out_specs=(spec,) * 3,
        scratch_shapes=[
            vm((ROWS, DT), BF16),
            vm((DT, COLS), BF16),
            vm((DS, COLS), BF16),
            vm((ROWS, DS), BF16),
            vm((ROWS, DS), BF16),
            vm((DS, ROWS), BF16),
            vm((ROWS, COLS), F32),
            vm((ROWS, COLS), F32),
            vm((ROWS, COLS), F32),
            vm((ROWS, COLS), BF16),
            vm((ROWS, 128), F32),
            vm((ROWS, 128), F32),
            vm((ROWS, 128), F32),
            vm((ROWS, 128), F32),
            vm((3, 1, COLS), F32),
            vm((3, 15, 1, COLS), F32),
            vm((2, 1, ROWS), F32),
            vm((2, 31, 1, ROWS), F32),
            vm((1, 2 * ROWS), F32),
            vm((31, 1, 2 * ROWS), F32),
            vm((2, 1, 128), F32),
            vm((31, 1, 128), F32),
            vm((15, 1, 128), F32),
            vm((256, DS), BF16),
            vm((256, DS), F32),
            vm((256, DS), BF16),
            vm((3, 64, DS), BF16),
            vm((3, 64, DS), BF16),
            vm((3, 16, DS), BF16),
            vm((3, 16, DS), BF16),
            vm((16, DS), BF16),
            vm((ROWS, DS), BF16),
            vm((4, 3, 256, 256), BF16),
            vm((4, 256, 256), F32),
            vm((4, 3, 256, 256), BF16),
            vm((4, 3, 64, 256), BF16),
            vm((4, 64, 256), F32),
            vm((4, 3, 64, 256), BF16),
            pltpu.SemaphoreType.DMA((NSEM,)),
            pltpu.SemaphoreType.DMA((NSEM,)),
        ],
        compiler_params=pltpu.CompilerParams(
            collective_id=0, has_side_effects=True, vmem_limit_bytes=56 * 2**20
        ),
    )(teacher_feats, teacher_weight, student_feats, student_weight)
    return (loss[0, 0], grad_weight, grad_feats)


def solution(mesh):
    return jax.shard_map(
        shards,
        mesh=mesh,
        in_specs=(P("batch", None), P("batch", "proto"), P("batch", None), P("batch", "proto")),
        out_specs=(P(), P("batch", "proto"), P("batch", None)),
        check_vma=False,
    )
```

time: 1060 us -> 171 us (0.16)
  blocking collectives: 531 us -> 0 us
  waiting for transfers between devices: 484 us -> 0 us
  Pallas kernels: 0 us -> 165 us
  matrix products: 14.6 us -> 0 us
  other arithmetic: 14.3 us -> 0 us
  between operations: 15.6 us -> 2.39 us
    psum x8 -> x0, blocking collectives: 531 us -> none  [the longest x3 233 us: shards(): row_total = lax.psum(jnp.sum(mass, axis=1), 'proto')]
    psum x1 -> x0, waiting for transfers between devices: 180 us -> none  [shards(): back = lax.psum(partial_back, 'proto')]
    pallas_call x0 -> x1, Pallas kernels: none -> 165 us  [shards(): pl.pallas_call(kernel, out_shape=(jax.ShapeDtypeStruct((1, 128), F32), ja...]
    reduce_scatter x1 -> x0, waiting for transfers between devices: 156 us -> none  [shards(): lax.psum_scatter(lax.dot_general(columns, slope, (((0,), (0,)), ((), ()))...]
    all_gather x2 -> x0, waiting for transfers between devices: 121 us -> none  [the longest x1 121 us: shards(): lax.all_gather(teacher_weight, 'batch', axis=0, tiled=True)]
    ppermute x1 -> x0, waiting for transfers between devices: 25.4 us -> none  [swapped(): lax.ppermute(x, axis, [(i, i ^ 1 << bit) for i in range(lax.axis_size(axi...]
    dot_general x4 -> x0, matrix products: 14.6 us -> none  [the longest x1 4.46 us: shards(): jnp.dot(student_half, weight_full, preferred_element_type=jnp.float32)]
  transfers between devices with their start and end apart: 5 -> 0, of which waited for: 4 -> 0; matrix products, arithmetic and copies ran while one was open for 2% -> 0% of each run, Pallas kernels for 0% -> 0%
where the time goes in v1:
time: 171 us
  Pallas kernels  165 us (96%)
  local copies, waits for them, and re-layouts  3.83 us (2%)
  between operations  2.39 us (1%)
    pallas_call x1, Pallas kernels, shards(): pl.pallas_call(kernel, out_shape=(jax.ShapeDtypeStruct((1, 128), F32), ja...  165 us
    unnamed x2, local copies, waits for them, and re-layouts  3.83 us

profile of v1, /device:TPU:1, one launch (start us, length us, event | category | flops | bytes accessed | tf_op | source)
XLA Modules:
  0.0 170.7 jit_solution(17821081857799124324)
XLA Ops:
  0.6 164.5 %shard_map.67 = (f32[1,128]{1,0:T(1,128)}, bf16[64,1024]{1,0:T(8,128)(2,1)}, bf16[512,1024]{1,0:T(8,128)(2,1)}) custom-call(bf16[512,1536]{1,0:T(8,128)(2,1)} %tf.1, bf16[96,1024]{1,0:T(8,128)(2,1)} %tw.1, bf16[512,1024]{1,0:T(8,128)(2,1)} %sf.1, bf16[64,1024]{1,0:T(8,128)(2,1)} %sw.1), custom_call_target="tpu_custom_call" | custom-call | tf_op jit(solution)/shard_map/pallas_call | solution.py:547
  165.8 1.6 copy.11
  167.3 2.3 %copy.12 = bf16[512,1024]{1,0:T(8,128)(2,1)} copy(bf16[512,1024]{1,0:T(8,128)(2,1)} %get-tuple-element.14) | data formatting | bytes 2097152

commit v2 on v1

--- a/solution.py
+++ b/solution.py
@@ -20,7 +20,8 @@
 COLS = 1024
 DT = 1536
 DS = 1024
-NSEM = 160
+NSEM = 256
+TPIECE = 1024
 
 
 def device(y, zh, x, zl, c):
@@ -52,7 +53,7 @@
     colmsg, colbuf, rowmsg, rowbuf, lastmsg, lastbuf,
     lossmsg, lossrow, losscol,
     bsend, bown, brecv, xsend, xrecv, lsend, lrecv, gfin, gfs,
-    gsend, gown, grecv, zsend, zown, zrecv,
+    gsend, gkeep, gown, grecv, zsend, zrecv,
     ssem, rsem,
 ):
     b = lax.axis_index("batch")
@@ -134,49 +135,74 @@
     wt[own(b, 96), :] = tw[...]
     ws[own(b, 64), :] = sw[...]
     pl.semaphore_wait(barrier, len(near))
-
-    def gather(full, rows):
+    def gather(full, rows, width):
         half = rows // 2
 
-        def part(dy, dz, h):
+        def part(dy, dz, h, k):
             start = (at_y(dy) * 4 + at_zh(dz)) * rows + h * half
-            return full.at[pl.ds(pl.multiple_of(start, 16), half), :]
-
-        zcopy, ycopy = {}, {}
-
-        def zsend_(dz_src, h, way):
-            ref = part(0, dz_src, h)
-            zcopy[(dz_src, h, way)] = single(ref, ref, device(y, at_zh(way), x, zl, c))
-
-        def ysend_(dy_src, dz, h, way):
-            ref = part(dy_src, dz, h)
-            ycopy[(dy_src, dz, h, way)] = single(ref, ref, device(at_y(way), zh, x, zl, c))
-
-        return zsend_, ysend_, zcopy, ycopy
-
-    tz, ty, tzc, tyc = gather(wt, 96)
-    sz, sy, szc, syc = gather(ws, 64)
-
-    def y_both(ysend_, dz):
-        for h in (0, 1):
-            ysend_(0, dz, h, 1)
-            ysend_(0, dz, h, 3)
-
-    def y_forward(ysend_, yc, dz, h):
-        if h == 0:
-            yc[(0, dz, 0, 1)].wait_recv()
-            ysend_(3, dz, 0, 1)
-        else:
-            yc[(0, dz, 1, 3)].wait_recv()
-            ysend_(1, dz, 1, 3)
-
-    tz(0, 0, 1)
-    tz(0, 1, 3)
-    tz(0, 1, 1)
-    tz(0, 0, 3)
+            return full.at[pl.ds(pl.multiple_of(start, 16), half), pl.ds(k * width, width)]
+
+        zc, yc = {}, {}
+        ks = range(COLS // width)
+
+        def zs(dz, h, way, k):
+            ref = part(0, dz, h, k)
+            zc[dz, h, way, k] = single(ref, ref, device(y, at_zh(way), x, zl, c))
+
+        def ys(dy, dz, h, way, k):
+            ref = part(dy, dz, h, k)
+            yc[dy, dz, h, way, k] = single(ref, ref, device(at_y(way), zh, x, zl, c))
+
+        def start():
+            for way, h in ((1, 0), (3, 1), (1, 1), (3, 0)):
+                for k in ks:
+                    zs(0, h, way, k)
+
+        def both(dz, h, k):
+            ys(0, dz, h, 1, k)
+            ys(0, dz, h, 3, k)
+
+        def forward(dz, h, k):
+            way, source = ((1, 3), (3, 1))[h]
+            yc[0, dz, h, way, k].wait_recv()
+            ys(source, dz, h, way, k)
+
+        def first(h, k):
+            way, source = ((1, 3), (3, 1))[h]
+            zc[0, h, way, k].wait_recv()
+            both(source, h, k)
+            zs(source, h, way, k)
+
+        def second(h, k):
+            way, source = ((3, 1), (1, 3))[h]
+            zc[0, h, way, k].wait_recv()
+            both(source, h, k)
+
+        def third(h, k):
+            way, source = ((1, 3), (3, 1))[h]
+            zc[source, h, way, k].wait_recv()
+            both(2, h, k)
+
+        def finish():
+            for dz in (0, 3, 1, 2):
+                for k in ks:
+                    yc[0, dz, 1, 1, k].wait_recv()
+                    yc[0, dz, 0, 3, k].wait_recv()
+                    yc[3, dz, 0, 1, k].wait_recv()
+                    yc[1, dz, 1, 3, k].wait_recv()
+
+        return start, both, forward, first, second, third, finish
+
+    t_start, t_both, t_forward, t_first, t_second, t_third, t_finish = gather(wt, 96, TPIECE)
+    s_start, s_both, s_forward, s_first, s_second, s_third, s_finish = gather(ws, 64, COLS)
+    tks = range(COLS // TPIECE)
+
+    for k in tks:
+        t_both(0, 0, k)
+        t_both(0, 1, k)
+    t_start()
     slice_rows = pl.ds(pl.multiple_of((2 * x + c) * 64, 64), 64)
     swap = single(sf.at[slice_rows, :], sf2.at[slice_rows, :], device(at_y(2), zh, x, zl, c))
-    y_both(ty, 0)
 
     def teacher_rows(i, carry):
         rows = pl.ds(pl.multiple_of(i * 128, 128), 128)
@@ -199,59 +225,28 @@
     rest = sf2.at[pl.ds(0, 448), :]
     pending.append(lambda: wait_bytes(rest, ssem.at[s_feats]))
 
-    y_forward(ty, tyc, 0, 0)
-    y_forward(ty, tyc, 0, 1)
-    tzc[(0, 0, 1)].wait_recv()
-    tz(3, 0, 1)
-    ty(0, 3, 0, 1)
-    ty(0, 3, 0, 3)
-    tzc[(0, 1, 3)].wait_recv()
-    tz(1, 1, 3)
-    ty(0, 1, 1, 1)
-    ty(0, 1, 1, 3)
-    sz(0, 0, 1)
-    sz(0, 1, 3)
-    sz(0, 1, 1)
-    sz(0, 0, 3)
-    y_forward(ty, tyc, 3, 0)
-    y_forward(ty, tyc, 1, 1)
-    tzc[(0, 1, 1)].wait_recv()
-    ty(0, 3, 1, 1)
-    ty(0, 3, 1, 3)
-    tzc[(0, 0, 3)].wait_recv()
-    ty(0, 1, 0, 1)
-    ty(0, 1, 0, 3)
-    y_forward(ty, tyc, 3, 1)
-    y_forward(ty, tyc, 1, 0)
-    tzc[(3, 0, 1)].wait_recv()
-    ty(0, 2, 0, 1)
-    ty(0, 2, 0, 3)
-    tzc[(1, 1, 3)].wait_recv()
-    ty(0, 2, 1, 1)
-    ty(0, 2, 1, 3)
-    y_both(sy, 0)
-
-    wait_bytes(rest, rsem.at[s_feats])
-
-    def student_rows(i, carry):
-        rows = pl.ds(pl.multiple_of(i * 128, 128), 128)
-        wide = sf2[rows, :].astype(F32)
-        scale = lax.rsqrt(jnp.sum(wide * wide, axis=1, keepdims=True) + 1e-06)
-        unit = wide * scale
-        sh[rows, :] = unit.astype(BF16)
-        sht[:, rows] = unit.T.astype(BF16)
-        return carry
-
-    lax.fori_loop(0, 4, student_rows, 0)
-
-    y_forward(ty, tyc, 2, 0)
-    y_forward(ty, tyc, 2, 1)
-    for dz in (0, 3, 1, 2):
-        tyc[(0, dz, 1, 1)].wait_recv()
-        tyc[(0, dz, 0, 3)].wait_recv()
-        tyc[(3, dz, 0, 1)].wait_recv()
-        tyc[(1, dz, 1, 3)].wait_recv()
-
+    for k in tks:
+        t_forward(0, 0, k)
+        t_forward(0, 1, k)
+    for k in tks:
+        t_first(0, k)
+        t_first(1, k)
+    for k in tks:
+        t_forward(3, 0, k)
+        t_forward(1, 1, k)
+    for k in tks:
+        t_second(1, k)
+        t_second(0, k)
+    for k in tks:
+        t_third(0, k)
+        t_third(1, k)
+        t_forward(3, 1, k)
+        t_forward(1, 0, k)
+    s_start()
+    for k in tks:
+        t_forward(2, 0, k)
+        t_forward(2, 1, k)
+    t_finish()
     def score_cols(j, carry):
         cols = pl.ds(pl.multiple_of(j * 256, 256), 256)
         scores = jnp.dot(tu[...], wt[:, cols], preferred_element_type=F32)
@@ -299,6 +294,15 @@
     def total_of(msg, buf):
         return msg + jnp.sum(buf[...], axis=0)
 
+    def student_rows(i, carry):
+        rows = pl.ds(pl.multiple_of(i * 128, 128), 128)
+        wide = sf2[rows, :].astype(F32)
+        scale = lax.rsqrt(jnp.sum(wide * wide, axis=1, keepdims=True) + 1e-06)
+        unit = wide * scale
+        sh[rows, :] = unit.astype(BF16)
+        sht[:, rows] = unit.T.astype(BF16)
+        return carry
+
     def student_logits():
         def body(j, carry):
             cols = pl.ds(pl.multiple_of(j * 256, 256), 256)
@@ -313,48 +317,38 @@
         lax.fori_loop(0, 4, body, 0)
 
     def student_near():
-        szc[(0, 0, 1)].wait_recv()
-        sz(3, 0, 1)
-        szc[(0, 1, 3)].wait_recv()
-        sz(1, 1, 3)
-        for dz, h in ((3, 0), (1, 1)):
-            sy(0, dz, h, 1)
-            sy(0, dz, h, 3)
-        y_forward(sy, syc, 0, 0)
-        y_forward(sy, syc, 0, 1)
-        szc[(0, 1, 1)].wait_recv()
-        szc[(0, 0, 3)].wait_recv()
-        for dz, h in ((3, 1), (1, 0)):
-            sy(0, dz, h, 1)
-            sy(0, dz, h, 3)
+        s_first(0, 0)
+        s_first(1, 0)
+        s_forward(0, 0, 0)
+        s_forward(0, 1, 0)
+        s_second(1, 0)
+        s_second(0, 0)
 
     def student_far():
-        szc[(3, 0, 1)].wait_recv()
-        szc[(1, 1, 3)].wait_recv()
-        y_both(sy, 2)
-        y_forward(sy, syc, 3, 0)
-        y_forward(sy, syc, 1, 1)
-        y_forward(sy, syc, 3, 1)
-        y_forward(sy, syc, 1, 0)
+        s_third(0, 0)
+        s_third(1, 0)
+        s_forward(3, 0, 0)
+        s_forward(1, 1, 0)
+        s_forward(3, 1, 0)
+        s_forward(1, 0, 0)
 
     def student_last():
-        y_forward(sy, syc, 2, 0)
-        y_forward(sy, syc, 2, 1)
+        s_forward(2, 0, 0)
+        s_forward(2, 1, 0)
 
     def student_end():
-        for dz in (0, 3, 1, 2):
-            syc[(0, dz, 1, 1)].wait_recv()
-            syc[(0, dz, 0, 3)].wait_recv()
-            syc[(3, dz, 0, 1)].wait_recv()
-            syc[(1, dz, 1, 3)].wait_recv()
+        s_finish()
         student_logits()
-
     for step in range(3):
         got = batch_send(colmsg.at[step], colbuf.at[step])
         if step == 0:
+            s_both(0, 0, 0)
+            s_both(0, 1, 0)
+            wait_bytes(rest, rsem.at[s_feats])
+            lax.fori_loop(0, 4, student_rows, 0)
             student_near()
         if step == 1:
-            student_last()
+            student_far()
         if step == 2:
             student_end()
             lastmsg[:, 512:] = lanes(totpart[...])
@@ -368,8 +362,8 @@
         if step < 2:
             rowmsg[step] = row_sum
             got = proto_send(rowmsg.at[step], rowbuf.at[step])
-            if step == 0:
-                student_far()
+            if step == 1:
+                student_last()
             got()
             row_total = total_of(rowmsg[step], rowbuf.at[step])
             colmsg[step + 1] = by_rows(1.0 / (CROPS * row_total))
@@ -384,7 +378,6 @@
     rowb[...] = jnp.broadcast_to(target_factor, (128, ROWS)).T
     probb[...] = jnp.broadcast_to(weight_sum * inverse(total, GAIN), (128, ROWS)).T
     crop_term = jnp.sum(weight_sum * jnp.log(total), axis=1, keepdims=True) / 32.0
-
     def slope_rows(i, carry):
         rows = pl.ds(pl.multiple_of(i * 64, 64), 64)
         by, prob = rowb[rows, :], probb[rows, :]
@@ -398,7 +391,6 @@
     pairs = lax.fori_loop(0, 8, slope_rows, jnp.zeros((8, 128), F32))
     pairs = jnp.sum(jnp.sum(pairs, axis=0, keepdims=True), axis=1, keepdims=True)
     lossmsg[0] = jnp.broadcast_to(crop_term - pairs, (1, 128))
-
     def back_half(half, store):
         rows = pl.ds(pl.multiple_of(half * 256, 256), 256)
 
@@ -418,24 +410,41 @@
     back_half(1 - c, store_send)
     core_copy = single(bsend, brecv, device(y, zh, x, zl, 1 - c))
 
-    ycopies = []
-    for q in range(4):
+    up, down = device(at_y(1), zh, x, zl, c), device(at_y(3), zh, x, zl, c)
+    ysent, yfwd, zcopies = {}, {}, []
+
+    def weight_made(q):
         cols = slice(256 * q, 256 * q + 256)
-        copies = []
         for dy in (2, 1, 3, 0):
             rows = pl.ds(pl.multiple_of(at_y(dy) * 256, 256), 256)
             value = jnp.dot(sht[rows, :], slope[:, cols], preferred_element_type=F32)
-            if dy:
-                gsend[q, dy - 1] = value.astype(BF16)
-                copies.append(
-                    single(gsend.at[q, dy - 1], grecv.at[q, dy - 1], device(at_y(dy), zh, x, zl, c))
-                )
+            if dy == 2:
+                gsend[q, 0] = value[:128].astype(BF16)
+                gsend[q, 1] = value[128:].astype(BF16)
+            elif dy == 1:
+                gkeep[q, 0] = value[:128]
+                gsend[q, 2] = value[128:].astype(BF16)
+            elif dy == 3:
+                gsend[q, 3] = value[:128].astype(BF16)
+                gkeep[q, 1] = value[128:]
             else:
                 gown[q] = value
-        ycopies.append(copies)
-        if q == 0:
-            back_half(c, store_own)
-
+
+    def weight_send(q):
+        ysent[q] = [
+            single(gsend.at[q, i], grecv.at[q, i], (up, down)[i % 2]) for i in range(4)
+        ]
+
+    def weight_forward(q):
+        for i in range(2):
+            ysent[q][i].wait_recv()
+            gsend[q, 4 + i] = (gkeep[q, i] + grecv[q, i].astype(F32)).astype(BF16)
+            yfwd[q, i] = single(gsend.at[q, 4 + i], grecv.at[q, 4 + i], (up, down)[i])
+
+    weight_made(0)
+    weight_send(0)
+    back_half(c, store_own)
+    weight_made(1)
     loss_got = proto_send(lossmsg.at[0], lossrow)
 
     core_copy.wait_recv()
@@ -445,27 +454,31 @@
         xsend[d - 1] = (bown[rows, :] + brecv[rows, :].astype(F32)).astype(BF16)
         xcopies.append(single(xsend.at[d - 1], xrecv.at[d - 1], device(y, zh, at_x(d), zl, c)))
 
-    zcopies = []
-
     def weight_z(q):
-        for copy in ycopies[q]:
-            copy.wait_recv()
+        ysent[q][2].wait_recv()
+        ysent[q][3].wait_recv()
+        yfwd[q, 0].wait_recv()
+        yfwd[q, 1].wait_recv()
+        low = gown[q, :128] + grecv[q, 3].astype(F32) + grecv[q, 4].astype(F32)
+        high = gown[q, 128:] + grecv[q, 2].astype(F32) + grecv[q, 5].astype(F32)
+        gown[q, :128] = low
+        gown[q, 128:] = high
         copies = []
-        for dz in (2, 1, 3, 0):
+        for dz in (2, 1, 3):
             rows = pl.ds(pl.multiple_of(at_zh(dz) * 64, 64), 64)
-            value = gown[q, rows, :]
-            for d in range(3):
-                value = value + grecv[q, d, rows, :].astype(F32)
-            if dz:
-                zsend[q, dz - 1] = value.astype(BF16)
-                copies.append(
-                    single(zsend.at[q, dz - 1], zrecv.at[q, dz - 1], device(y, at_zh(dz), x, zl, c))
-                )
-            else:
-                zown[q] = value
+            zsend[q, dz - 1] = gown[q, rows, :].astype(BF16)
+            copies.append(
+                single(zsend.at[q, dz - 1], zrecv.at[q, dz - 1], device(y, at_zh(dz), x, zl, c))
+            )
         zcopies.append(copies)
 
+    weight_forward(0)
+    weight_send(1)
+    weight_made(2)
     weight_z(0)
+    weight_forward(1)
+    weight_send(2)
+    weight_made(3)
 
     for copy in xcopies:
         copy.wait_recv()
@@ -480,8 +493,9 @@
         rows = pl.ds(pl.multiple_of(fl * 16, 16), 16)
         lsend[d - 1] = bown[rows, :].astype(BF16)
         lcopies.append(single(lsend.at[d - 1], lrecv.at[d - 1], device(y, zh, x, fl, c)))
-
     weight_z(1)
+    weight_forward(2)
+    weight_send(3)
     loss_got()
     lossmsg[1] = lossmsg[0] + jnp.sum(lossrow[...], axis=0)
     loss_got = batch_send(lossmsg.at[1], losscol)
@@ -502,8 +516,8 @@
     for d in range(4):
         fl = lax.rem(zl + d, 4)
         fcopies.append(single(gfin, gfs.at[mine, :], device(at_y(2), zh, x, fl, c)))
-
     weight_z(2)
+    weight_forward(3)
 
     for copy in fcopies:
         copy.wait_recv()
@@ -515,7 +529,6 @@
     for d in (2, 1, 3):
         lastx.append(single(piece(0, c), piece(0, c), device(y, zh, at_x(d), zl, c)))
     lastc = [single(piece(0, c), piece(0, c), device(y, zh, x, zl, 1 - c))]
-
     weight_z(3)
 
     for d, copy in zip((2, 1, 3), lastx):
@@ -526,11 +539,10 @@
         cols = slice(256 * q, 256 * q + 256)
         for copy in zcopies[q]:
             copy.wait_recv()
-        value = zown[q]
+        value = gown[q, pl.ds(pl.multiple_of(zh * 64, 64), 64), :]
         for d in range(3):
             value = value + zrecv[q, d].astype(F32)
         gw_out[:, cols] = value.astype(BF16)
-
     loss_got()
     loss_out[...] = (lossmsg[1] + jnp.sum(losscol[...], axis=0)) / CROPS
 
@@ -586,11 +598,11 @@
             vm((3, 16, DS), BF16),
             vm((16, DS), BF16),
             vm((ROWS, DS), BF16),
-            vm((4, 3, 256, 256), BF16),
+            vm((4, 6, 128, 256), BF16),
+            vm((4, 2, 128, 256), F32),
             vm((4, 256, 256), F32),
-            vm((4, 3, 256, 256), BF16),
+            vm((4, 6, 128, 256), BF16),
             vm((4, 3, 64, 256), BF16),
-            vm((4, 64, 256), F32),
             vm((4, 3, 64, 256), BF16),
             pltpu.SemaphoreType.DMA((NSEM,)),
             pltpu.SemaphoreType.DMA((NSEM,)),

time: 171 us -> 164 us (0.959)
  Pallas kernels: 165 us -> 158 us
    pallas_call x1, Pallas kernels: 165 us -> 158 us  [shards(): pl.pallas_call(kernel, out_shape=(jax.ShapeDtypeStruct((1, 128), F32), ja...]
where the time goes in v2:
time: 164 us
  Pallas kernels  158 us (96%)
  local copies, waits for them, and re-layouts  3.83 us (2%)
  between operations  2.39 us (1%)
    pallas_call x1, Pallas kernels, shards(): pl.pallas_call(kernel, out_shape=(jax.ShapeDtypeStruct((1, 128), F32), ja...  158 us
    unnamed x2, local copies, waits for them, and re-layouts  3.83 us

profile of v2, /device:TPU:1, one launch (start us, length us, event | category | flops | bytes accessed | tf_op | source)
XLA Modules:
  0.0 163.8 jit_solution(8885102645078695297)
XLA Ops:
  0.6 157.5 %shard_map.67 = (f32[1,128]{1,0:T(1,128)}, bf16[64,1024]{1,0:T(8,128)(2,1)}, bf16[512,1024]{1,0:T(8,128)(2,1)}) custom-call(bf16[512,1536]{1,0:T(8,128)(2,1)} %tf.1, bf16[96,1024]{1,0:T(8,128)(2,1)} %tw.1, bf16[512,1024]{1,0:T(8,128)(2,1)} %sf.1, bf16[64,1024]{1,0:T(8,128)(2,1)} %sw.1), custom_call_target="tpu_custom_call" | custom-call | tf_op jit(solution)/shard_map/pallas_call | solution.py:559
  158.8 1.6 copy.11
  160.4 2.3 %copy.12 = bf16[512,1024]{1,0:T(8,128)(2,1)} copy(bf16[512,1024]{1,0:T(8,128)(2,1)} %get-tuple-element.14) | data formatting | bytes 2097152

commit v3 on v2

--- a/solution.py
+++ b/solution.py
@@ -47,14 +47,15 @@
 
 
 def kernel(
-    tf, tw, sf, sw, loss_out, gw_out, gf_out,
+    tf_in, tw, sf, sw, loss_out, gw_out, gf_out,
+    tf,
     tu, wt, ws, sf2, sh, sht, mass, logit, expo, slope,
     rowpart, totpart, rowb, probb,
     colmsg, colbuf, rowmsg, rowbuf, lastmsg, lastbuf,
     lossmsg, lossrow, losscol,
     bsend, bown, brecv, xsend, xrecv, lsend, lrecv, gfin, gfs,
     gsend, gkeep, gown, grecv, zsend, zrecv,
-    ssem, rsem,
+    ssem, rsem, isem,
 ):
     b = lax.axis_index("batch")
     p = lax.axis_index("proto")
@@ -69,6 +70,9 @@
 
     def at_x(d):
         return lax.rem(x + d, 4)
+
+    fetch = pltpu.make_async_copy(tf_in, tf, isem)
+    fetch.start()
 
     used = [0]
     pending = []
@@ -203,6 +207,8 @@
     t_start()
     slice_rows = pl.ds(pl.multiple_of((2 * x + c) * 64, 64), 64)
     swap = single(sf.at[slice_rows, :], sf2.at[slice_rows, :], device(at_y(2), zh, x, zl, c))
+
+    fetch.wait()
 
     def teacher_rows(i, carry):
         rows = pl.ds(pl.multiple_of(i * 128, 128), 128)
@@ -411,7 +417,7 @@
     core_copy = single(bsend, brecv, device(y, zh, x, zl, 1 - c))
 
     up, down = device(at_y(1), zh, x, zl, c), device(at_y(3), zh, x, zl, c)
-    ysent, yfwd, zcopies = {}, {}, []
+    ysent, yfwd = {}, {}
 
     def weight_made(q):
         cols = slice(256 * q, 256 * q + 256)
@@ -454,6 +460,12 @@
         xsend[d - 1] = (bown[rows, :] + brecv[rows, :].astype(F32)).astype(BF16)
         xcopies.append(single(xsend.at[d - 1], xrecv.at[d - 1], device(y, zh, at_x(d), zl, c)))
 
+    front, rear = device(y, at_zh(1), x, zl, c), device(y, at_zh(3), x, zl, c)
+    zsent, zfwd = {}, {}
+
+    def weight_piece(q, dz, h):
+        return gown[q, pl.ds(pl.multiple_of(at_zh(dz) * 64 + h * 32, 32), 32), :]
+
     def weight_z(q):
         ysent[q][2].wait_recv()
         ysent[q][3].wait_recv()
@@ -463,14 +475,18 @@
         high = gown[q, 128:] + grecv[q, 2].astype(F32) + grecv[q, 5].astype(F32)
         gown[q, :128] = low
         gown[q, 128:] = high
-        copies = []
-        for dz in (2, 1, 3):
-            rows = pl.ds(pl.multiple_of(at_zh(dz) * 64, 64), 64)
-            zsend[q, dz - 1] = gown[q, rows, :].astype(BF16)
-            copies.append(
-                single(zsend.at[q, dz - 1], zrecv.at[q, dz - 1], device(y, at_zh(dz), x, zl, c))
-            )
-        zcopies.append(copies)
+        for i, (dz, h) in enumerate(((2, 0), (2, 1), (1, 1), (3, 0))):
+            zsend[q, i] = weight_piece(q, dz, h).astype(BF16)
+        zsent[q] = [
+            single(zsend.at[q, i], zrecv.at[q, i], (front, rear)[i % 2]) for i in range(4)
+        ]
+
+    def weight_pass(q):
+        for i in range(2):
+            zsent[q][i].wait_recv()
+            kept = weight_piece(q, (1, 3)[i], i)
+            zsend[q, 4 + i] = (kept + zrecv[q, i].astype(F32)).astype(BF16)
+            zfwd[q, i] = single(zsend.at[q, 4 + i], zrecv.at[q, 4 + i], (front, rear)[i])
 
     weight_forward(0)
     weight_send(1)
@@ -516,8 +532,10 @@
     for d in range(4):
         fl = lax.rem(zl + d, 4)
         fcopies.append(single(gfin, gfs.at[mine, :], device(at_y(2), zh, x, fl, c)))
+    weight_pass(0)
     weight_z(2)
     weight_forward(3)
+    weight_pass(1)
 
     for copy in fcopies:
         copy.wait_recv()
@@ -530,19 +548,24 @@
         lastx.append(single(piece(0, c), piece(0, c), device(y, zh, at_x(d), zl, c)))
     lastc = [single(piece(0, c), piece(0, c), device(y, zh, x, zl, 1 - c))]
     weight_z(3)
+    weight_pass(2)
 
     for d, copy in zip((2, 1, 3), lastx):
         copy.wait_recv()
         lastc.append(single(piece(4 - d, c), piece(4 - d, c), device(y, zh, x, zl, 1 - c)))
 
+    weight_pass(3)
     for q in range(4):
         cols = slice(256 * q, 256 * q + 256)
-        for copy in zcopies[q]:
-            copy.wait_recv()
-        value = gown[q, pl.ds(pl.multiple_of(zh * 64, 64), 64), :]
-        for d in range(3):
-            value = value + zrecv[q, d].astype(F32)
-        gw_out[:, cols] = value.astype(BF16)
+        zsent[q][2].wait_recv()
+        zsent[q][3].wait_recv()
+        zfwd[q, 0].wait_recv()
+        zfwd[q, 1].wait_recv()
+        low = weight_piece(q, 0, 0) + zrecv[q, 3].astype(F32) + zrecv[q, 4].astype(F32)
+        high = weight_piece(q, 0, 1) + zrecv[q, 2].astype(F32) + zrecv[q, 5].astype(F32)
+        gw_out[:32, cols] = low.astype(BF16)
+        gw_out[32:, cols] = high.astype(BF16)
+
     loss_got()
     loss_out[...] = (lossmsg[1] + jnp.sum(losscol[...], axis=0)) / CROPS
 
@@ -556,16 +579,18 @@
 def shards(teacher_feats, teacher_weight, student_feats, student_weight):
     vm = pltpu.VMEM
     spec = pl.BlockSpec(memory_space=pltpu.VMEM)
+    away = pl.BlockSpec(memory_space=pl.ANY)
     loss, grad_weight, grad_feats = pl.pallas_call(
         kernel,
         out_shape=(
             jax.ShapeDtypeStruct((1, 128), F32),
-            jax.ShapeDtypeStruct((64, COLS), BF16),
-            jax.ShapeDtypeStruct((ROWS, DS), BF16),
+            vm((64, COLS), BF16),
+            vm((ROWS, DS), BF16),
         ),
-        in_specs=[spec] * 4,
+        in_specs=[away, spec, away, spec],
         out_specs=(spec,) * 3,
         scratch_shapes=[
+            vm((ROWS, DT), BF16),
             vm((ROWS, DT), BF16),
             vm((DT, COLS), BF16),
             vm((DS, COLS), BF16),
@@ -602,10 +627,11 @@
             vm((4, 2, 128, 256), F32),
             vm((4, 256, 256), F32),
             vm((4, 6, 128, 256), BF16),
-            vm((4, 3, 64, 256), BF16),
-            vm((4, 3, 64, 256), BF16),
+            vm((4, 6, 32, 256), BF16),
+            vm((4, 6, 32, 256), BF16),
             pltpu.SemaphoreType.DMA((NSEM,)),
             pltpu.SemaphoreType.DMA((NSEM,)),
+            pltpu.SemaphoreType.DMA,
         ],
         compiler_params=pltpu.CompilerParams(
             collective_id=0, has_side_effects=True, vmem_limit_bytes=56 * 2**20

time: 164 us -> 157 us (0.957)
  the two profiles are of different devices: /device:TPU:1 before, /device:TPU:4 now
where the time goes in v3:
time: 157 us
  Pallas kernels  153 us (97%)
  between operations  1.81 us (1%)
  local copies, waits for them, and re-layouts  1.63 us (1%)
    pallas_call x1, Pallas kernels, shards(): pl.pallas_call(kernel, out_shape=(jax.ShapeDtypeStruct((1, 128), F32), vm...  153 us

profile of v3, /device:TPU:4, one launch (start us, length us, event | category | flops | bytes accessed | tf_op | source)
XLA Modules:
  0.0 156.7 jit_solution(9123506905791301473)
XLA Ops:
  0.6 153.3 %shard_map.67 = (f32[1,128]{1,0:T(1,128)}, bf16[64,1024]{1,0:T(8,128)(2,1)S(1)}, bf16[512,1024]{1,0:T(8,128)(2,1)S(1)}) custom-call(bf16[512,1536]{1,0:T(8,128)(2,1)} %tf_in.1, bf16[96,1024]{1,0:T(8,128)(2,1)} %tw.1, bf16[512,1024]{1,0:T(8,128)(2,1)} %sf.1, bf16[64,1024]{1,0:T(8,128)(2,1)} %sw.1), custom_call_target="tpu_custom_call" | custom-call | tf_op jit(solution)/shard_map/pallas_call | solution.py:583
  153.9 0.0 copy-start
  153.9 0.7 copy.10
  154.6 1.0 copy.11
  155.5 0.0 copy-done
Async XLA Ops:
  153.9 1.6 %copy-start = (f32[1,128]{1,0:T(1,128)S(1)}, f32[1,128]{1,0:T(1,128)}, u32[]{:S(2)}) copy-start(f32[1,128]{1,0:T(1,128)} %get-tuple-element.6) | copy-start | bytes 1540

commit v4 on v3

--- a/solution.py
+++ b/solution.py
@@ -244,14 +244,15 @@
         t_second(1, k)
         t_second(0, k)
     for k in tks:
+        t_forward(3, 1, k)
+        t_forward(1, 0, k)
+    for k in tks:
         t_third(0, k)
         t_third(1, k)
-        t_forward(3, 1, k)
-        t_forward(1, 0, k)
-    s_start()
     for k in tks:
         t_forward(2, 0, k)
         t_forward(2, 1, k)
+    s_start()
     t_finish()
     def score_cols(j, carry):
         cols = pl.ds(pl.multiple_of(j * 256, 256), 256)
@@ -451,7 +452,6 @@
     weight_send(0)
     back_half(c, store_own)
     weight_made(1)
-    loss_got = proto_send(lossmsg.at[0], lossrow)
 
     core_copy.wait_recv()
     xcopies = []
@@ -459,6 +459,8 @@
         rows = pl.ds(pl.multiple_of(at_x(d) * 64, 64), 64)
         xsend[d - 1] = (bown[rows, :] + brecv[rows, :].astype(F32)).astype(BF16)
         xcopies.append(single(xsend.at[d - 1], xrecv.at[d - 1], device(y, zh, at_x(d), zl, c)))
+
+    loss_got = proto_send(lossmsg.at[0], lossrow)
 
     front, rear = device(y, at_zh(1), x, zl, c), device(y, at_zh(3), x, zl, c)
     zsent, zfwd = {}, {}
@@ -512,9 +514,6 @@
     weight_z(1)
     weight_forward(2)
     weight_send(3)
-    loss_got()
-    lossmsg[1] = lossmsg[0] + jnp.sum(lossrow[...], axis=0)
-    loss_got = batch_send(lossmsg.at[1], losscol)
 
     for copy in lcopies:
         copy.wait_recv()
@@ -532,6 +531,9 @@
     for d in range(4):
         fl = lax.rem(zl + d, 4)
         fcopies.append(single(gfin, gfs.at[mine, :], device(at_y(2), zh, x, fl, c)))
+    loss_got()
+    lossmsg[1] = lossmsg[0] + jnp.sum(lossrow[...], axis=0)
+    loss_got = batch_send(lossmsg.at[1], losscol)
     weight_pass(0)
     weight_z(2)
     weight_forward(3)

time: 157 us -> 159 us (1.013)
  the two profiles are of different devices: /device:TPU:4 before, /device:TPU:1 now
where the time goes in v4:
time: 159 us; the launch traced here: 158 us
  Pallas kernels  154 us (97%)
  between operations  1.81 us (1%)
  local copies, waits for them, and re-layouts  1.63 us (1%)
    pallas_call x1, Pallas kernels, shards(): pl.pallas_call(kernel, out_shape=(jax.ShapeDtypeStruct((1, 128), F32), vm...  154 us

profile of v4, /device:TPU:1, one launch (start us, length us, event | category | flops | bytes accessed | tf_op | source)
XLA Modules:
  0.0 157.8 jit_solution(9251945855522869469)
XLA Ops:
  0.6 154.3 %shard_map.67 = (f32[1,128]{1,0:T(1,128)}, bf16[64,1024]{1,0:T(8,128)(2,1)S(1)}, bf16[512,1024]{1,0:T(8,128)(2,1)S(1)}) custom-call(bf16[512,1536]{1,0:T(8,128)(2,1)} %tf_in.1, bf16[96,1024]{1,0:T(8,128)(2,1)} %tw.1, bf16[512,1024]{1,0:T(8,128)(2,1)} %sf.1, bf16[64,1024]{1,0:T(8,128)(2,1)} %sw.1), custom_call_target="tpu_custom_call" | custom-call | tf_op jit(solution)/shard_map/pallas_call | solution.py:585
  155.0 0.0 copy-start
  155.0 0.7 copy.10
  155.6 1.0 copy.11
  156.6 0.0 copy-done
Async XLA Ops:
  155.0 1.6 %copy-start = (f32[1,128]{1,0:T(1,128)S(1)}, f32[1,128]{1,0:T(1,128)}, u32[]{:S(2)}) copy-start(f32[1,128]{1,0:T(1,128)} %get-tuple-element.6) | copy-start | bytes 1540
